TPU v7x, 32 devices: a whole 2x2x4 slice. The times are simulated.
32 devices in a mesh: row: 4 (over y, x), col: 8 (over z, core).
Axes of the slice: x: 2, y: 2, z: 4, core: 2. Of those that a mesh axis runs over, the one named last changes fastest.
Arguments:
- state: float32 [3, 10, 131072], P(None, None, ('row', 'col')), may hold values from -6 to 6
- depth: float32 [131072], P(('row', 'col')), may hold values from 1 to 18
- metric: float32 [4, 131072], P(None, ('row', 'col')), may hold values from -4 to 4, as said below
- partner: int32 [131072], P(('row', 'col')), may hold values from -63 to 63, as said below
- refine: int32 [131072], P(('row', 'col')), may hold values from 0 to 1, as said below
- diff_ops: float32 [2, 10, 10], replicated, may hold values from -2 to 2
- lift: float32 [10, 12], replicated, may hold values from -1.75 to 1.75
- prolong: float32 [2, 10, 10], replicated, may hold values from -2 to 2
Outputs:
- refined: float32 [3, 10, 196608], P(None, None, ('row', 'col'))
Inputs may be any that keep to these rules, and one draw needn't show every extreme that they name: `metric`: (r_x, r_y) and (s_x, s_y) are orthogonal and of equal length, between 1 and 4. Where partner[i] is not 0, j = i + partner[i] is a triangle with partner[j] = -partner[i]; an offset of size 63 occurs in every draw. `refine`: split the curve into sections of 4096 consecutive triangles. The refinements before section k number k * 2048 plus an offset between -1024 and 1024, and both ends of that range occur in every draw; all refinements together number 131072 / 2.
All inputs are finite; a program needn't handle non-finite values.
Results may differ from a plain program's by a relative error of at most 0.000076.
Values sent between devices are 32-bit elements; how exact they have to be, the bound alone decides.
No kernel may reach another device: no remote copies, remote signals or barrier semaphores. Data moves between devices by JAX's collectives and lax.ppermute only.
A program may use at most 64 MiB of HBM per device.

v0:
```python
import jax
import jax.numpy as jnp
from jax import lax
from jax.sharding import PartitionSpec as P

RIM = 64


GRAVITY = 9.81
COURANT = 0.5
HIGH = lax.Precision.HIGHEST


def padded(cells, sides, width):
    for axis, dim in sides:
        count = lax.axis_size(axis)
        ends = count - 1
        head = lax.slice_in_dim(cells, 0, width, axis=dim)
        tail = lax.slice_in_dim(cells, cells.shape[dim] - width, cells.shape[dim], axis=dim)
        cells = jnp.concatenate(
            [
                lax.ppermute(tail, axis, [(i, (i + 1) % count) for i in range(ends)]),
                cells,
                lax.ppermute(head, axis, [((i + 1) % count, i) for i in range(ends)]),
            ],
            axis=dim,
        )
    return cells


def entering(value, axis, join, neutral):
    count, mine = (lax.axis_size(axis), lax.axis_index(axis))
    pieces = lax.all_gather(value, axis)
    total = jnp.full_like(value, 0) + jnp.asarray(neutral, value.dtype)

    def hop(position, total):
        longer = join(total, pieces[position])
        return jnp.where(position < mine, longer, total)

    return lax.fori_loop(0, count - 1, hop, total)


def shifted(block, axis, distance):
    devices = range(lax.axis_size(axis))
    route = [(i - distance, i) for i in devices if i - distance in devices]
    return lax.ppermute(block, axis, route)


def apply_ops(matrix, field):
    return jnp.einsum("ab,fbx->fax", matrix, field, precision=HIGH)


def face_rows(field):
    return jnp.concatenate(
        [
            field[:, 0:4],
            field[:, 3:4],
            field[:, 6:7],
            field[:, 8:10],
            field[:, 9:10],
            field[:, 7:8],
            field[:, 4:5],
            field[:, 0:1],
        ],
        axis=1,
    )


def normal_flux(values, speed_sq, normal_x, normal_y):
    return jnp.stack(
        [
            values[1] * normal_x + values[2] * normal_y,
            speed_sq * values[0] * normal_x,
            speed_sq * values[0] * normal_y,
        ]
    )


def face_vectors(metric):
    grad_rx, grad_ry, grad_sx, grad_sy = (metric[0], metric[1], metric[2], metric[3])
    return ((-grad_sx, -grad_sy), (grad_rx + grad_sx, grad_ry + grad_sy), (-grad_rx, -grad_ry))


def wave_rate(depth, metric):
    lengths = [jnp.sqrt(vx * vx + vy * vy) for vx, vy in face_vectors(metric)]
    return jnp.sqrt(GRAVITY * depth) * jnp.maximum(jnp.maximum(lengths[0], lengths[1]), lengths[2])


def tendency(state, depth, metric, outer, outer_depth, walls, diff_ops, lift):
    speed_sq = GRAVITY * depth
    grad_rx, grad_ry, grad_sx, grad_sy = (metric[0], metric[1], metric[2], metric[3])
    moved = jnp.stack([state[1], state[2], state[0]])
    along_r = apply_ops(diff_ops[0], moved)
    along_s = apply_ops(diff_ops[1], moved)
    vol_eta = -(
        grad_rx * along_r[0] + grad_sx * along_s[0] + grad_ry * along_r[1] + grad_sy * along_s[1]
    )
    vol_mx = -speed_sq * (grad_rx * along_r[2] + grad_sx * along_s[2])
    vol_my = -speed_sq * (grad_ry * along_r[2] + grad_sy * along_s[2])
    inner = face_rows(state)
    jumps = []
    for edge_num, (vec_x, vec_y) in enumerate(face_vectors(metric)):
        length = jnp.sqrt(vec_x * vec_x + vec_y * vec_y)
        normal_x = vec_x / length
        normal_y = vec_y / length
        inside = inner[:, 4 * edge_num : 4 * edge_num + 4, :]
        normal_m = inside[1] * normal_x + inside[2] * normal_y
        ghost = jnp.stack(
            [
                inside[0],
                inside[1] - 2.0 * normal_m * normal_x,
                inside[2] - 2.0 * normal_m * normal_y,
            ]
        )
        closed = walls[edge_num]
        outside = jnp.where(closed, ghost, outer[edge_num])
        outside_sq = jnp.where(closed, speed_sq, GRAVITY * outer_depth[edge_num])
        flux_in = normal_flux(inside, speed_sq, normal_x, normal_y)
        flux_out = normal_flux(outside, outside_sq, normal_x, normal_y)
        wave_top = jnp.sqrt(jnp.maximum(speed_sq, outside_sq))
        common = 0.5 * (flux_in + flux_out) - 0.5 * wave_top * (outside - inside)
        jumps.append(length * (flux_in - common))
    surface = apply_ops(lift, jnp.concatenate(jumps, axis=1))
    return jnp.stack([vol_eta, vol_mx, vol_my]) + surface


def add_ints(earlier, later):
    return earlier + later


def window_rows(data, start):
    return lax.dynamic_slice_in_dim(data, start, 128, data.ndim - 1)


def shards(state, depth, metric, partner, refine, diff_ops, lift, prolong):
    cells = state.shape[2]
    nblocks = cells // 128
    reach = 128 + 2 * RIM
    devices = lax.axis_size(("row", "col"))
    place = lax.axis_index(("row", "col"))
    first_cell = place * cells
    index = first_cell + jnp.arange(cells, dtype=jnp.int32)
    top = lax.pmax(jnp.max(wave_rate(depth, metric)), ("row", "col"))
    step = COURANT / top
    walls = (index == 0, index == devices * cells - 1, partner == 0)
    pair_local = jnp.arange(128, dtype=jnp.int32)[None, :] + partner.reshape(nblocks, 128) + RIM

    def neighbours(payload):
        return padded(payload, ((("row", "col"), 1),), RIM)

    def rhs(current):
        own_traces = face_rows(current)
        flat = jnp.concatenate([own_traces.reshape(36, cells), depth[None, :]], axis=0)
        wide = neighbours(flat)
        traces = wide[:36].reshape(3, 12, cells + 2 * RIM)
        depth_wide = wide[36]
        from_prev = traces[:, 7:3:-1, RIM - 1 : RIM - 1 + cells]
        from_next = traces[:, 3::-1, RIM + 1 : RIM + 1 + cells]
        depth_prev = depth_wide[RIM - 1 : RIM - 1 + cells]
        depth_next = depth_wide[RIM + 1 : RIM + 1 + cells]
        pair_src = jnp.concatenate(
            [traces[:, 11:7:-1, :].reshape(12, cells + 2 * RIM), depth_wide[None, :]], axis=0
        )
        main_part = pair_src[:, :cells].reshape(13, nblocks, 128)
        rest = pair_src[:, 128:]
        rest = jnp.concatenate([rest, jnp.zeros((13, 128 - 2 * RIM), jnp.float32)], axis=1)
        tail_part = rest.reshape(13, nblocks, 128)
        windows = jnp.concatenate([main_part, tail_part], axis=2)
        pair_table = (
            pair_local[:, :, None] == lax.broadcasted_iota(jnp.int32, (nblocks, 128, reach), 2)
        ).astype(jnp.float32)
        picked = jnp.einsum("rbw,bjw->rbj", windows, pair_table, precision=HIGH).reshape(13, cells)
        from_pair = picked[:12].reshape(3, 4, cells)
        depth_pair = picked[12]
        return tendency(
            current,
            depth,
            metric,
            (from_prev, from_next, from_pair),
            (depth_prev, depth_next, depth_pair),
            walls,
            diff_ops,
            lift,
        )

    first = state + step * rhs(state)
    second = 0.5 * state + 0.5 * (first + step * rhs(first))
    counts = 1 + refine
    blocks = counts.reshape(-1, 128).astype(jnp.float32)
    row_ids = lax.broadcasted_iota(jnp.int32, (128, 128), 0)
    col_ids = lax.broadcasted_iota(jnp.int32, (128, 128), 1)
    upper = (row_ids <= col_ids).astype(jnp.float32)
    within = jnp.dot(blocks, upper, precision=HIGH, preferred_element_type=jnp.float32)
    block_sums = within[:, -1]
    before = jnp.cumsum(block_sums) - block_sums
    ends = (within + before[:, None]).reshape(-1).astype(jnp.int32)
    starts = ends - counts
    extra = jnp.sum(refine)
    earlier = entering(extra, ("row", "col"), add_ints, jnp.int32(0))
    margin = cells // 4
    share = 3 * cells // 2
    span = share + 2 * margin
    slot_blocks = (span + 127) // 128
    offset = earlier - place * (cells // 2) + margin
    bases = jnp.arange(slot_blocks, dtype=jnp.int32) * 128 - offset
    first_parent = jnp.searchsorted(ends, bases, side="right", method="compare_all")
    win_start = jnp.clip(first_parent, 0, cells - 128)
    child_one = jnp.where(refine == 1, apply_ops(prolong[0], second), second).reshape(30, cells)
    child_two = apply_ops(prolong[1], second).reshape(30, cells)
    data = jnp.concatenate([child_one, child_two], axis=0)
    lanes = jnp.arange(128, dtype=jnp.int32)
    iota_pick = lax.broadcasted_iota(jnp.int32, (128, 128), 1)

    def place_block(inputs):
        base, begin = inputs
        data_win = window_rows(data, begin)
        ends_win = window_rows(ends, begin)
        starts_win = window_rows(starts, begin)
        slots = base + lanes
        local = jnp.sum((ends_win[None, :] <= slots[:, None]).astype(jnp.int32), axis=1)
        local = jnp.minimum(local, 127)
        hit = local[:, None] == iota_pick
        which = slots[:, None] - starts_win[None, :]
        pick_one = (hit & (which == 0)).astype(jnp.float32)
        pick_two = (hit & (which == 1)).astype(jnp.float32)
        return jnp.einsum("ri,pi->rp", data_win[:30], pick_one, precision=HIGH) + jnp.einsum(
            "ri,pi->rp", data_win[30:], pick_two, precision=HIGH
        )

    placed = lax.map(place_block, (bases, win_start))
    canvas = jnp.transpose(placed, (1, 0, 2)).reshape(3, 10, slot_blocks * 128)
    flat_slots = (bases[:, None] + lanes[None, :]).reshape(-1)
    valid = (flat_slots >= 0) & (flat_slots < ends[-1])
    canvas = jnp.where(valid, canvas, 0.0)
    from_after = shifted(canvas[:, :, :margin], ("row", "col"), -1)
    from_before = shifted(canvas[:, :, margin + share :], ("row", "col"), 1)
    middle = canvas[:, :, margin : margin + share]
    middle = middle.at[:, :, share - margin :].add(from_after)
    middle = middle.at[:, :, :margin].add(from_before)
    return middle


def solution(mesh):
    return jax.shard_map(
        shards,
        mesh=mesh,
        in_specs=(
            P(None, None, ("row", "col")),
            P(("row", "col")),
            P(None, ("row", "col")),
            P(("row", "col")),
            P(("row", "col")),
            P(),
            P(),
            P(),
        ),
        out_specs=P(None, None, ("row", "col")),
        check_vma=False,
    )
```

profile of v0, /device:TPU:4, one launch (start us, length us, event | category | flops | bytes accessed | tf_op | source)
XLA Modules:
  0.0 682.5 jit_solution(1812125264548315387)
XLA Ops:
  0.0 1.4 copy.79
  3.3 1.9 collective-permute-start
  5.3 7.4 %collective-permute-start.1 = (f32[37,64]{1,0:T(8,128)}, f32[37,64]{1,0:T(8,128)}, u32[]{:S(2)}, u32[]{:S(2)}) collective-permute-start(f32[37,64]{1,0:T(8,128)} %get-tuple-element.264), channel_id=1, source_target_pairs={{1,0},{2,1},{3,2},{4,3},{5,4},{6,5},{7,6},{8,7},{9,8},{10,9},{11,1... | collective-permute-start | bytes 28424 | tf_op jit(solution)/shard_map/ppermute | solution.py:24
  21.5 1.8 convolution_bitcast_fusion.7
  24.9 2.1 add_subtract_fusion
  27.9 37.7 %all-reduce = s32[32]{0:T(128)S(1)} all-reduce(s32[32]{0:T(128)S(1)} %dynamic-update-slice.6), channel_id=1, replica_groups=mesh['row'=4,'col'=8] {'row','col'}, use_global_device_ids=true, to_apply=%add | all-reduce | flops 32 | bytes 256
  65.5 34.9 %while.26 = (s32[]{:T(128)}, s32[]{:T(128)}, s32[]{:T(128)}, s32[32]{0:T(128)S(1)}, s32[]{:T(128)}) while((s32[]{:T(128)}, s32[]{:T(128)}, s32[]{:T(128)}, s32[32]{0:T(128)S(1)}, s32[]{:T(128)}) %tuple.151), condition=%wide.region_2.3_spmd, body=%wide.region_1.0_spmd.sunk | while | flops 5 | bytes 107 | solution.py:40
  104.9 2.2 concatenate.71
  108.0 2.0 reshape.981
  111.1 2.3 fusion.154
  115.2 2.5 fusion.36
  119.1 9.8 %rev.18 = f32[3,4,4096]{2,1,0:T(4,128)} reverse(f32[3,4,4096]{2,1,0:T(4,128)S(1)} %copy-done.40), dimensions={1} | reverse | bytes 393216 | tf_op jit(solution)/shard_map/rev | solution.py:157
  130.0 1.7 copy.74
  133.6 2.2 sqrt_multiply_fusion.5
  135.8 42.9 %pmax.7 = f32[]{:T(128)} all-reduce(f32[]{:T(128)} %get-tuple-element.322), channel_id=1, replica_groups=mesh['row'=4,'col'=8] {'row','col'}, use_global_device_ids=true, to_apply=%region_6.7 | all-reduce | flops 1 | bytes 8 | tf_op jit(solution)/shard_map/pmax | solution.py:143
  178.8 1.5 multiply_subtract_fusion.11
  189.7 1.5 fusion.69
  196.2 1.7 convolution_bitcast_fusion.3
  199.1 4.1 concatenate.79
  204.5 2.0 collective-permute-start.2
  206.6 7.5 %collective-permute-start.3 = (f32[37,64]{1,0:T(8,128)S(1)}, f32[37,64]{1,0:T(8,128)}, u32[]{:S(2)}, u32[]{:S(2)}) collective-permute-start(f32[37,64]{1,0:T(8,128)S(1)} %get-tuple-element.260), channel_id=1, source_target_pairs={{1,0},{2,1},{3,2},{4,3},{5,4},{6,5},{7,6},{8,7},{9,8},{10,9},{11,1... | collective-permute-start | bytes 28424 | tf_op jit(solution)/shard_map/ppermute | solution.py:24
  214.1 1.5 multiply_subtract_fusion.3
  216.2 1.4 fusion.158
  222.8 2.2 fusion.153
  229.0 2.5 fusion.37
  242.1 423.4 %while.27 = (s32[]{:T(128)}, f32[64,30,128]{2,1,0:T(8,128)}, s32[64]{0:T(128)S(1)}, f32[60,4096]{1,0:T(8,128)S(1)}, s32[4096]{0:T(1024)}, /*index=5*/s32[64]{0:T...) while((s32[]{:T(128)}, f32[64,30,128]{2,1,0:T(8,128)}, ...), condition=%wide.region_9.10_spmd.clone, body=%wide.region_7.9_spmd.clone.sunk | while | flops 11980678 | bytes 89803 | solution.py:230
  665.4 1.8 copy.82
  668.1 2.2 collective-permute-start.4
  670.4 2.1 collective-permute-start.5
  672.5 1.4 collective-permute-done.4
  674.0 7.0 %collective-permute-done.5 = f32[3,10,1024]{2,1,0:T(8,128)S(1)} collective-permute-done((f32[3,10,1024]{2,1,0:T(8,128)S(1)}, f32[3,10,1024]{2,1,0:T(8,128)S(1)}, u32[]{:S(2)}, u32[]{:S(2)}) %collective-permute-start.5) | collective-permute-done | bytes 122912 | tf_op jit(solution)/shard_map/ppermute | solution.py:46
  681.0 1.5 copy.83
  (1081 shorter events, 375.6 us)
Async XLA Ops:
  0.0 192.1 %copy-start = (f32[10,12]{1,0:T(8,128)S(1)}, f32[10,12]{1,0:T(8,128)}, u32[]{:S(2)}) copy-start(f32[10,12]{1,0:T(8,128)} %param.22) | copy-start | bytes 1444
  1.7 11.9 %copy-start.14 = (f32[3,1,4096]{2,1,0:T(1,128)}, f32[3,1,4096]{2,1,0:T(1,128)S(1)}, u32[]{:S(2)}) copy-start(f32[3,1,4096]{2,1,0:T(1,128)S(1)} %get-tuple-element.253) | copy-start | bytes 147460
  3.3 101.5 %collective-permute-start = (f32[37,64]{1,0:T(8,128)}, f32[37,64]{1,0:T(8,128)}, u32[]{:S(2)}, u32[]{:S(2)}) collective-permute-start(f32[37,64]{1,0:T(8,128)} %get-tuple-element.265), channel_id=1, source_target_pairs={{0,1},{1,2},{2,3},{3,4},{4,5},{5,6},{6,7},{7,8},{8,9},{9,10},{10,1... | collective-permute-start | bytes 28424 | tf_op jit(solution)/shard_map/ppermute | solution.py:22
  5.3 99.6 %collective-permute-start.1 = (f32[37,64]{1,0:T(8,128)}, f32[37,64]{1,0:T(8,128)}, u32[]{:S(2)}, u32[]{:S(2)}) collective-permute-start(f32[37,64]{1,0:T(8,128)} %get-tuple-element.264), channel_id=1, source_target_pairs={{1,0},{2,1},{3,2},{4,3},{5,4},{6,5},{7,6},{8,7},{9,8},{10,9},{11,1... | collective-permute-start | bytes 28424 | tf_op jit(solution)/shard_map/ppermute | solution.py:24
  27.1 80.9 %copy-start.162 = (s32[4096]{0:T(1024)}, s32[4096]{0:T(1024)S(1)}, u32[]{:S(2)}) copy-start(s32[4096]{0:T(1024)S(1)} %get-tuple-element.425) | copy-start | bytes 49156
  104.0 87.2 %copy-start.146 = (pred[4096]{0:T(1024)(128)(4,1)}, pred[4096]{0:T(1024)(128)(4,1)S(1)}, u32[]{:S(2)}) copy-start(pred[4096]{0:T(1024)(128)(4,1)S(1)} %get-tuple-element.335) | copy-start | bytes 12292
  104.8 83.5 %copy-start.107 = (f32[1,4096]{1,0:T(1,128)}, f32[1,4096]{1,0:T(1,128)S(1)}, u32[]{:S(2)}) copy-start(f32[1,4096]{1,0:T(1,128)S(1)} %slice.498) | copy-start | bytes 49156
  114.8 14.1 %copy-start.39 = (f32[3,4,4096]{2,1,0:T(4,128)S(1)}, f32[3,4,4096]{2,1,0:T(4,128)}, u32[]{:S(2)}) copy-start(f32[3,4,4096]{2,1,0:T(4,128)} %get-tuple-element.238) | copy-start | bytes 589828
  115.2 17.4 %copy-start.13 = (f32[4096]{0:T(1024)S(1)}, f32[4096]{0:T(1024)}, u32[]{:S(2)}) copy-start(f32[4096]{0:T(1024)} %param.17) | copy-start | bytes 49156
  118.5 15.1 %copy-start.41 = (f32[1,4096]{1,0:T(1,128)S(1)}, f32[1,4096]{1,0:T(1,128)}, u32[]{:S(2)}) copy-start(f32[1,4096]{1,0:T(1,128)} %get-tuple-element.307) | copy-start | bytes 49156
  118.5 60.2 %copy-start.57 = (f32[1,4096]{1,0:T(1,128)S(1)}, f32[1,4096]{1,0:T(1,128)}, u32[]{:S(2)}) copy-start(f32[1,4096]{1,0:T(1,128)} %copy-done.56) | copy-start | bytes 49156
  118.5 60.2 %copy-start.61 = (f32[1,4096]{1,0:T(1,128)S(1)}, f32[1,4096]{1,0:T(1,128)}, u32[]{:S(2)}) copy-start(f32[1,4096]{1,0:T(1,128)} %copy-done.60) | copy-start | bytes 49156
  132.7 50.2 %copy-start.49 = (f32[1,4096]{1,0:T(1,128)S(1)}, f32[1,4096]{1,0:T(1,128)}, u32[]{:S(2)}) copy-start(f32[1,4096]{1,0:T(1,128)} %copy-done.48) | copy-start | bytes 49156
  132.7 50.2 %copy-start.53 = (f32[1,4096]{1,0:T(1,128)S(1)}, f32[1,4096]{1,0:T(1,128)}, u32[]{:S(2)}) copy-start(f32[1,4096]{1,0:T(1,128)} %copy-done.52) | copy-start | bytes 49156
  133.6 49.3 %copy-start.8 = (f32[3,4,4096]{2,1,0:T(4,128)S(1)}, f32[3,4,4096]{2,1,0:T(4,128)}, u32[]{:S(2)}) copy-start(f32[3,4,4096]{2,1,0:T(4,128)} %get-tuple-element.333) | copy-start | bytes 589828
  133.6 49.3 %copy-start.140 = (f32[4096]{0:T(1024)S(1)}, f32[4096]{0:T(1024)}, u32[]{:S(2)}) copy-start(f32[4096]{0:T(1024)} %broadcast_multiply_fusion.3) | copy-start | bytes 49156
  199.0 15.0 %copy-start.50 = (f32[1,4096]{1,0:T(1,128)S(1)}, f32[1,4096]{1,0:T(1,128)}, u32[]{:S(2)}) copy-start(f32[1,4096]{1,0:T(1,128)} %copy-done.48) | copy-start | bytes 49156
  199.1 15.0 %copy-start.54 = (f32[1,4096]{1,0:T(1,128)S(1)}, f32[1,4096]{1,0:T(1,128)}, u32[]{:S(2)}) copy-start(f32[1,4096]{1,0:T(1,128)} %copy-done.52) | copy-start | bytes 49156
  203.2 14.4 %copy-start.42 = (f32[1,4096]{1,0:T(1,128)S(1)}, f32[1,4096]{1,0:T(1,128)}, u32[]{:S(2)}) copy-start(f32[1,4096]{1,0:T(1,128)} %get-tuple-element.307) | copy-start | bytes 49156
  203.2 14.4 %copy-start.46 = (f32[1,4096]{1,0:T(1,128)S(1)}, f32[1,4096]{1,0:T(1,128)}, u32[]{:S(2)}) copy-start(f32[1,4096]{1,0:T(1,128)} %copy-done.44) | copy-start | bytes 49156
  204.4 13.2 %copy-start.139 = (f32[4096]{0:T(1024)S(1)}, f32[4096]{0:T(1024)}, u32[]{:S(2)}) copy-start(f32[4096]{0:T(1024)} %get-tuple-element.337) | copy-start | bytes 49156
  204.4 13.9 %copy-start.145 = (f32[4096]{0:T(1024)S(1)}, f32[4096]{0:T(1024)}, u32[]{:S(2)}) copy-start(f32[4096]{0:T(1024)} %broadcast_multiply_fusion) | copy-start | bytes 49156
  204.4 14.6 %copy-start.2 = (f32[3,10,4096]{2,1,0:T(8,128)S(1)}, f32[3,10,4096]{2,1,0:T(8,128)}, u32[]{:S(2)}) copy-start(f32[3,10,4096]{2,1,0:T(8,128)} %convolution_bitcast_fusion.3) | copy-start | bytes 1474564
  204.4 14.6 %copy-start.108 = (f32[1,4096]{1,0:T(1,128)S(1)}, f32[1,4096]{1,0:T(1,128)}, u32[]{:S(2)}) copy-start(f32[1,4096]{1,0:T(1,128)} %copy-done.107) | copy-start | bytes 49156
  204.4 14.6 %copy-start.110 = (f32[1,4096]{1,0:T(1,128)S(1)}, f32[1,4096]{1,0:T(1,128)}, u32[]{:S(2)}) copy-start(f32[1,4096]{1,0:T(1,128)} %get-tuple-element.310) | copy-start | bytes 49156
  204.4 14.6 %copy-start.112 = (f32[1,4096]{1,0:T(1,128)S(1)}, f32[1,4096]{1,0:T(1,128)}, u32[]{:S(2)}) copy-start(f32[1,4096]{1,0:T(1,128)} %get-tuple-element.311) | copy-start | bytes 49156
  204.4 14.6 %copy-start.114 = (f32[1,4096]{1,0:T(1,128)S(1)}, f32[1,4096]{1,0:T(1,128)}, u32[]{:S(2)}) copy-start(f32[1,4096]{1,0:T(1,128)} %get-tuple-element.312) | copy-start | bytes 49156
  204.4 14.6 %copy-start.137 = (f32[4096]{0:T(1024)S(1)}, f32[4096]{0:T(1024)}, u32[]{:S(2)}) copy-start(f32[4096]{0:T(1024)} %get-tuple-element.326) | copy-start | bytes 49156
  204.5 15.5 %collective-permute-start.2 = (f32[37,64]{1,0:T(8,128)S(1)}, f32[37,64]{1,0:T(8,128)S(1)}, u32[]{:S(2)}, u32[]{:S(2)}) collective-permute-start(f32[37,64]{1,0:T(8,128)S(1)} %get-tuple-element.261), channel_id=1, source_target_pairs={{0,1},{1,2},{2,3},{3,4},{4,5},{5,6},{6,7},{7,8},{8,9},{9,10},{10,1... | collective-permute-start | bytes 28424 | tf_op jit(solution)/shard_map/ppermute | solution.py:22
  206.6 14.1 %collective-permute-start.3 = (f32[37,64]{1,0:T(8,128)S(1)}, f32[37,64]{1,0:T(8,128)}, u32[]{:S(2)}, u32[]{:S(2)}) collective-permute-start(f32[37,64]{1,0:T(8,128)S(1)} %get-tuple-element.260), channel_id=1, source_target_pairs={{1,0},{2,1},{3,2},{4,3},{5,4},{6,5},{7,6},{8,7},{9,8},{10,9},{11,1... | collective-permute-start | bytes 28424 | tf_op jit(solution)/shard_map/ppermute | solution.py:24
  668.1 5.9 collective-permute-start.4
  670.4 10.6 %collective-permute-start.5 = (f32[3,10,1024]{2,1,0:T(8,128)S(1)}, f32[3,10,1024]{2,1,0:T(8,128)S(1)}, u32[]{:S(2)}, u32[]{:S(2)}) collective-permute-start(f32[3,10,1024]{2,1,0:T(8,128)S(1)} %get-tuple-element.233), channel_id=1, source_target_pairs={{0,1},{1,2},{2,3},{3,4},{4,5},{5,6},{6,7},{7,8},{8,9},{9,10},{10,1... | collective-permute-start | bytes 368648 | tf_op jit(solution)/shard_map/ppermute | solution.py:46
  (148 other events, 454.5 us)
where the time goes:
time: 695 us; the launch traced here: 682 us
  local copies, waits for them, and re-layouts  245 us (35%)
  loops' own time  144 us (21%)
  other arithmetic  91.7 us (13%)
  matrix products  87 us (13%)
  blocking collectives  80.6 us (12%)
  starting transfers between devices  23.1 us (3%)
  waiting for transfers between devices  8.42 us (1%)
    another operation x1, loops' own time, shards(): placed = lax.map(place_block, (bases, win_start))  126 us
    dynamic_slice x128, local copies, waits for them, and re-layouts, window_rows(): return lax.dynamic_slice_in_dim(data, start, 128, data.ndim - 1)  98.6 us
    dynamic_slice x128, local copies, waits for them, and re-layouts, shards(): placed = lax.map(place_block, (bases, win_start))  74.5 us
    dot_general x64, matrix products, place_block(): jnp.einsum('ri,pi->rp', data_win[30:], pick_two, precision=HIGH)  59.2 us
    pmax x1, blocking collectives, shards(): top = lax.pmax(jnp.max(wave_rate(depth, metric)), ('row', 'col'))  42.9 us
    add x64, other arithmetic, place_block(): slots = base + lanes  41.4 us
    unnamed x1, blocking collectives  37.7 us
    another operation x1, loops' own time, entering(): return lax.fori_loop(0, count - 1, hop, total)  17.7 us
  transfers between devices with their start and end apart: 6, of which 2 were waited for; matrix products, arithmetic and copies ran while one was open for 6% of the time, Pallas kernels for 0%

commit v1 on v0

v1 whole, which is shorter than its diff:
```python
import functools

import jax
import jax.numpy as jnp
from jax import lax
from jax.experimental import pallas as pl
from jax.experimental.pallas import tpu as pltpu
from jax.sharding import PartitionSpec as P

GRAVITY = 9.81
COURANT = 0.5
HIGH = lax.Precision.HIGHEST
LANES = 128
AXES = ("row", "col")
FACES = ((0, 1, 2, 3), (3, 6, 8, 9), (9, 7, 4, 0))
PACK = 40
WIDE = 48
PAD = 8

VMEM = pl.BlockSpec(memory_space=pltpu.VMEM)
SMEM = pl.BlockSpec(memory_space=pltpu.SMEM)
PARAMS = pltpu.CompilerParams(vmem_limit_bytes=48 * 1024 * 1024)


class Sizes:
    def __init__(self, cells):
        self.cells = cells
        self.blocks = cells // LANES
        self.margin = cells // 4 // LANES
        self.halo = self.margin + 1
        self.pre = -(-self.halo // 8) * 8
        self.rows = self.blocks + 2 * self.pre
        self.tall = self.rows + 2 * PAD
        self.slots = 3 * self.blocks // 2
        self.keep = self.pre - self.margin


def split_metric(metric_ref, spread, blocks):
    for block in range(blocks):
        spread[8 * block : 8 * block + 4, :] = metric_ref[:, LANES * block : LANES * (block + 1)]
    return [spread[pl.ds(comp, blocks, stride=8), :] for comp in range(4)]


def pack_kernel(
    sizes, state_ref, depth_ref, metric_ref, partner_ref, refine_ref, stats_ref, head_ref, tail_ref, spread
):
    blocks, halo = sizes.blocks, sizes.halo
    rx, ry, sx, sy = split_metric(metric_ref, spread, blocks)
    depth = depth_ref[...]
    refine = refine_ref[...].astype(jnp.float32)
    faces = ((sx, sy), (rx + sx, ry + sy), (rx, ry))
    lengths = [jnp.sqrt(vx * vx + vy * vy) for vx, vy in faces]
    rate = jnp.sqrt(GRAVITY * depth) * jnp.maximum(jnp.maximum(lengths[0], lengths[1]), lengths[2])
    top = jnp.max(jnp.max(rate, axis=0, keepdims=True), axis=1, keepdims=True)
    extra = jnp.sum(jnp.sum(refine, axis=0, keepdims=True), axis=1, keepdims=True)
    shape = stats_ref.shape
    lane = lax.broadcasted_iota(jnp.int32, shape, 1)
    stats_ref[...] = jnp.where(
        lane < LANES // 2, jnp.broadcast_to(top, shape), jnp.broadcast_to(extra, shape)
    )
    partner = partner_ref[...].astype(jnp.float32)
    for ref, start in ((head_ref, 0), (tail_ref, blocks - halo)):
        for block in range(halo):
            lo = LANES * (start + block)
            for field in range(3):
                at = PACK * block + 10 * field
                ref[at : at + 10, :] = state_ref[field, :, lo : lo + LANES]
        for num, dense in enumerate((depth, rx, ry, sx, sy, partner, refine)):
            ref[pl.ds(30 + num, halo, stride=PACK), :] = dense[start : start + halo]


def pair_index(partner):
    lane = lax.broadcasted_iota(jnp.int32, partner.shape, 1)
    target = lane + partner.astype(jnp.int32)
    return target & (LANES - 1), (target >= 0) & (target < LANES)


def lane_gather(values, index):
    return jnp.take_along_axis(values, index, axis=1, mode="promise_in_bounds")


def outer_values(load, index, inside):
    shape = index.shape
    lane = lax.broadcasted_iota(jnp.int32, shape, 1)

    def prev(item):
        return pltpu.roll(jnp.where(lane == LANES - 1, load(item, -1), load(item, 0)), 1, 1)

    def after(item):
        return pltpu.roll(jnp.where(lane == 0, load(item, 1), load(item, 0)), LANES - 1, 1)

    def across(item):
        other = jnp.where(lane < LANES // 2, load(item, 1), load(item, -1))
        return jnp.where(inside, lane_gather(load(item, 0), index), lane_gather(other, index))

    return prev, after, across


def wall_masks(sizes, group, place, count, partner):
    shape = partner.shape
    lane = lax.broadcasted_iota(jnp.int32, shape, 1)
    row = lax.broadcasted_iota(jnp.int32, shape, 0) + 8 * group
    first = (lane == 0) & (row == sizes.pre) & (place == 0)
    last = (lane == LANES - 1) & (row == sizes.pre + sizes.blocks - 1) & (place == count - 1)
    return first, last, partner == 0


def tendency(load, geo, walls, index, inside, diff_ref, lift_ref):
    speed_sq, rx, ry, sx, sy = geo[:5]
    outer_sq, waves, ghosts = geo[5:8], geo[8:11], geo[11:14]
    own = [[load(10 * field + node, 0) for node in range(10)] for field in range(3)]
    eta, mom_x, mom_y = own
    flow_r = [-(rx * mom_x[b] + ry * mom_y[b]) for b in range(10)]
    flow_s = [-(sx * mom_x[b] + sy * mom_y[b]) for b in range(10)]
    half_r = (0.5 * rx, 0.5 * ry)
    half_s = (0.5 * sx, 0.5 * sy)
    vectors = (
        (-half_s[0], -half_s[1]),
        (half_r[0] + half_s[0], half_r[1] + half_s[1]),
        (-half_r[0], -half_r[1]),
    )
    fetch = outer_values(load, index, inside)
    jumps = ([], [], [])
    for face in range(3):
        vec_x, vec_y = vectors[face]
        theirs = FACES[(1, 0, 2)[face]]
        wall = walls[face]
        for j in range(4):
            node, match = FACES[face][j], theirs[3 - j]
            in_eta, in_x, in_y = eta[node], mom_x[node], mom_y[node]
            ext_eta, ext_x, ext_y = [fetch[face](10 * field + match) for field in range(3)]
            bounce = (in_x * vec_x + in_y * vec_y) * ghosts[face]
            d_eta = jnp.where(wall, 0.0, in_eta - ext_eta)
            d_x = jnp.where(wall, bounce * vec_x, in_x - ext_x)
            d_y = jnp.where(wall, bounce * vec_y, in_y - ext_y)
            head = jnp.where(wall, 0.0, speed_sq * in_eta - outer_sq[face] * ext_eta)
            jumps[0].append(d_x * vec_x + d_y * vec_y - waves[face] * d_eta)
            jumps[1].append(head * vec_x - waves[face] * d_x)
            jumps[2].append(head * vec_y - waves[face] * d_y)
    pull = (-speed_sq * rx, -speed_sq * ry)
    push = (-speed_sq * sx, -speed_sq * sy)
    out = [[None] * 10 for _ in range(3)]
    for a in range(10):
        total = along_r = along_s = None
        for b in range(10):
            d_r, d_s = diff_ref[0, a, b], diff_ref[1, a, b]
            term = d_r * flow_r[b] + d_s * flow_s[b]
            total = term if b == 0 else total + term
            along_r = d_r * eta[b] if b == 0 else along_r + d_r * eta[b]
            along_s = d_s * eta[b] if b == 0 else along_s + d_s * eta[b]
        sums = [total, pull[0] * along_r + push[0] * along_s, pull[1] * along_r + push[1] * along_s]
        for q in range(12):
            weight = lift_ref[a, q]
            for field in range(3):
                sums[field] = sums[field] + weight * jumps[field][q]
        for field in range(3):
            out[field][a] = sums[field]
    return [out[field][a] for field in range(3) for a in range(10)]


def first_kernel(
    sizes, state_ref, depth_ref, metric_ref, partner_ref, refine_ref, before_ref, after_ref, diff_ref, lift_ref,
    cur, rate_ref, geo_ref, spread, wide, aux,
):
    blocks, halo, pre = sizes.blocks, sizes.halo, sizes.pre
    top, bottom = PAD + pre, PAD + pre + blocks
    place = lax.axis_index(AXES)
    count = lax.axis_size(AXES)
    metric = split_metric(metric_ref, spread, blocks)
    dense = [depth_ref[...], *metric, partner_ref[...].astype(jnp.float32), refine_ref[...].astype(jnp.float32)]
    for num in range(7):
        aux[num, top - halo : top, :] = before_ref[pl.ds(30 + num, halo, stride=PACK), :]
        aux[num, top:bottom, :] = dense[num]
        aux[num, bottom : bottom + halo, :] = after_ref[pl.ds(30 + num, halo, stride=PACK), :]
    for block in range(blocks):
        for field in range(3):
            at = WIDE * block + 16 * field
            wide[at : at + 10, :] = state_ref[field, :, LANES * block : LANES * (block + 1)]
    for field in range(3):
        for node in range(10):
            item = 10 * field + node
            cur[item, top - halo : top, :] = before_ref[pl.ds(item, halo, stride=PACK), :]
            cur[item, top:bottom, :] = wide[pl.ds(16 * field + node, blocks, stride=WIDE), :]
            cur[item, bottom : bottom + halo, :] = after_ref[pl.ds(item, halo, stride=PACK), :]

    def step(group, carry):
        base = PAD + 8 * group

        def load_aux(item, shift):
            return aux[item, pl.ds(base + shift, 8), :]

        def load(item, shift):
            return cur[item, pl.ds(base + shift, 8), :]

        depth, rx, ry, sx, sy, partner, refine = [load_aux(num, 0) for num in range(7)]
        index, inside = pair_index(partner)
        fetch = outer_values(load_aux, index, inside)
        walls = wall_masks(sizes, group, place, count, partner)
        speed_sq = GRAVITY * depth
        outer_sq = [jnp.where(walls[k], speed_sq, GRAVITY * fetch[k](0)) for k in range(3)]
        faces = ((sx, sy), (rx + sx, ry + sy), (rx, ry))
        squares = [vx * vx + vy * vy for vx, vy in faces]
        waves = [
            0.5 * jnp.sqrt(squares[k]) * jnp.sqrt(jnp.maximum(speed_sq, outer_sq[k])) for k in range(3)
        ]
        ghosts = [8.0 / squares[k] for k in range(3)]
        geo = [speed_sq, rx, ry, sx, sy, *outer_sq, *waves, *ghosts]
        rates = tendency(load, geo, walls, index, inside, diff_ref, lift_ref)
        at = pl.ds(pl.multiple_of(8 * group, 8), 8)
        for num, value in enumerate([*geo, partner, refine]):
            geo_ref[num, at, :] = value
        for item in range(30):
            rate_ref[item, at, :] = rates[item]
        return carry

    lax.fori_loop(0, sizes.rows // 8, step, 0)


def second_kernel(
    sizes, cur, rate_ref, geo_ref, stats_ref, diff_ref, lift_ref, prolong_ref, out_ref,
    first, ends_ref, place_v, place_s, wide, weights, gathered, index_ref, sem,
):
    slots, keep, rows = sizes.slots, sizes.keep, sizes.rows
    place = lax.axis_index(AXES)
    count = lax.axis_size(AXES)
    stats = stats_ref[...]
    lane_n = lax.broadcasted_iota(jnp.int32, stats.shape, 1)
    dev_n = lax.broadcasted_iota(jnp.int32, stats.shape, 0)
    rate = jnp.where(lane_n < LANES // 2, stats, 0.0)
    top = jnp.max(jnp.max(rate, axis=0, keepdims=True), axis=1, keepdims=True)
    gone = jnp.where((lane_n == LANES - 1) & (dev_n < place), stats, 0.0)
    earlier = jnp.sum(jnp.sum(gone, axis=0, keepdims=True), axis=1, keepdims=True)
    step = COURANT / top
    wide[...] = jnp.zeros(wide.shape, jnp.float32)
    refine = geo_ref[15, keep : keep + slots, :]
    counts = (1.0 + refine).astype(jnp.bfloat16)
    row_i = lax.broadcasted_iota(jnp.int32, (LANES, LANES), 0)
    col_i = lax.broadcasted_iota(jnp.int32, (LANES, LANES), 1)
    upper = (row_i <= col_i).astype(jnp.bfloat16)
    within = jnp.dot(counts, upper, preferred_element_type=jnp.float32)
    whole = jnp.dot(counts, jnp.ones((LANES, LANES), jnp.bfloat16), preferred_element_type=jnp.float32)
    row_s = lax.broadcasted_iota(jnp.int32, (slots, slots), 0)
    col_s = lax.broadcasted_iota(jnp.int32, (slots, slots), 1)
    lower = (col_s < row_s).astype(jnp.bfloat16)
    before = jnp.dot(lower, whole.astype(jnp.bfloat16), preferred_element_type=jnp.float32)
    own = before[sizes.margin : sizes.margin + 1, :]
    start = earlier - (place * (sizes.cells // 2)).astype(jnp.float32)
    ends = within + before + (start - own)
    ends_ref[:slots, :] = 2.0 * ends + refine
    ends_ref[slots:, :] = jnp.full((8, LANES), 1e9, jnp.float32)
    full = before + whole + (start - own)
    first_slot = LANES * lax.broadcasted_iota(jnp.int32, (slots, LANES), 1).astype(jnp.float32)
    lead = jnp.sum((full <= first_slot).astype(jnp.float32), axis=0, keepdims=True)
    lead = jnp.clip(lead.astype(jnp.int32), 0, slots - 1)
    place_v[...] = jnp.broadcast_to(lead, (8, LANES))
    copy = pltpu.make_async_copy(place_v, place_s, sem)
    copy.start()

    for item in range(30):
        first[item, PAD : PAD + rows, :] = cur[item, PAD : PAD + rows, :] + step * rate_ref[item]

    def stage(group, carry):
        base = PAD + 8 * group
        at = pl.ds(pl.multiple_of(8 * group, 8), 8)

        def load(item, shift):
            return first[item, pl.ds(base + shift, 8), :]

        geo = [geo_ref[num, at, :] for num in range(14)]
        partner = geo_ref[14, at, :]
        index, inside = pair_index(partner)
        walls = wall_masks(sizes, group, place, count, partner)
        rates = tendency(load, geo, walls, index, inside, diff_ref, lift_ref)
        lead_row = (8 * group - keep) * WIDE
        for field in range(3):
            for node in range(10):
                item = 10 * field + node
                old = cur[item, pl.ds(pl.multiple_of(base, 8), 8), :]
                new = 0.5 * old + 0.5 * (load(item, 0) + step * rates[item])
                wide[pl.ds(lead_row + 16 * field + node, 8, stride=WIDE), :] = new
        return carry

    lax.fori_loop(keep // 8, (keep + slots) // 8, stage, 0)

    weights[...] = jnp.zeros(weights.shape, jnp.float32)
    for child in range(2):
        for field in range(3):
            weights[
                WIDE * child + 16 * field : WIDE * child + 16 * field + 10, 16 * field : 16 * field + 10
            ] = prolong_ref[child]
    copy.wait()
    for slot in range(slots):
        lead_at = place_s[0, slot]
        index_ref[0, slot : slot + 1, :] = ends_ref[pl.ds(lead_at, 1), :]
        index_ref[1, slot : slot + 1, :] = ends_ref[pl.ds(lead_at + 1, 1), :]
    near, far = index_ref[0], index_ref[1]
    slot_no = LANES * lax.broadcasted_iota(jnp.int32, (slots, LANES), 0) + lax.broadcasted_iota(
        jnp.int32, (slots, LANES), 1
    )
    goal = (2 * slot_no + 1).astype(jnp.float32)
    beyond = jnp.broadcast_to(near[:, LANES - 1 :], (slots, LANES)) <= goal

    def pick(index):
        return jnp.where(beyond, lane_gather(far, index), lane_gather(near, index))

    found = jnp.zeros((slots, LANES), jnp.int32)
    size = LANES // 2
    while size:
        passed = pick(found + (size - 1)) <= goal
        found = jnp.where(passed, found + size, found)
        size //= 2
    mine = pick(found).astype(jnp.int32)
    split = mine & 1
    begin = (mine >> 1) - 1 - split
    kind = split * (1 + slot_no - begin)
    index_ref[0] = found.astype(jnp.float32)
    index_ref[1] = kind.astype(jnp.float32)
    index_ref[2] = beyond.astype(jnp.float32)
    for slot in range(slots):
        lead_at = place_s[0, slot] * WIDE
        lane_idx = jnp.broadcast_to(index_ref[0, slot : slot + 1, :], (WIDE, LANES)).astype(jnp.int32)
        passed = jnp.broadcast_to(index_ref[2, slot : slot + 1, :], (WIDE, LANES)) > 0.5
        one = wide[pl.ds(pl.multiple_of(lead_at, WIDE), WIDE), :]
        two = wide[pl.ds(pl.multiple_of(lead_at + WIDE, WIDE), WIDE), :]
        gathered[:, LANES * slot : LANES * (slot + 1)] = jnp.where(
            passed, lane_gather(two, lane_idx), lane_gather(one, lane_idx)
        )
    matrix = weights[...]
    chunk = 8 * LANES
    for part in range(slots // 8):
        span = slice(chunk * part, chunk * (part + 1))
        values = gathered[:, span]
        children = jnp.dot(matrix, values, precision=HIGH, preferred_element_type=jnp.float32)
        for sub in range(8):
            slot = 8 * part + sub
            cut = slice(LANES * sub, LANES * (sub + 1))
            tag = jnp.broadcast_to(index_ref[1, slot : slot + 1, :], (16, LANES))
            for field in range(3):
                at = slice(16 * field, 16 * field + 16)
                second = slice(WIDE + 16 * field, WIDE + 16 * field + 16)
                value = jnp.where(
                    tag < 0.5,
                    values[at, cut],
                    jnp.where(tag < 1.5, children[at, cut], children[second, cut]),
                )
                out_ref[field, :, LANES * slot : LANES * (slot + 1)] = value[:10]


def shards(state, depth, metric, partner, refine, diff_ops, lift, prolong):
    sizes = Sizes(state.shape[2])
    count = lax.axis_size(AXES)
    blocks, rows, slots = sizes.blocks, sizes.rows, sizes.slots
    depth, partner, refine = [x.reshape(blocks, LANES) for x in (depth, partner, refine)]
    f32 = jnp.float32
    packed = jax.ShapeDtypeStruct((PACK * sizes.halo, LANES), f32)
    stats, head, tail = pl.pallas_call(
        functools.partial(pack_kernel, sizes),
        name="pack",
        out_shape=(jax.ShapeDtypeStruct((count, LANES), f32), packed, packed),
        in_specs=[VMEM] * 5,
        out_specs=(VMEM,) * 3,
        scratch_shapes=[pltpu.VMEM((8 * blocks, LANES), f32)],
        compiler_params=PARAMS,
    )(state, depth, metric, partner, refine)
    before = lax.ppermute(tail, AXES, [(i, (i + 1) % count) for i in range(count)])
    after = lax.ppermute(head, AXES, [((i + 1) % count, i) for i in range(count)])
    stats = lax.all_to_all(stats, AXES, 0, 0, tiled=True)
    cur, rates, geo = pl.pallas_call(
        functools.partial(first_kernel, sizes),
        name="first_stage",
        out_shape=(
            jax.ShapeDtypeStruct((30, sizes.tall, LANES), f32),
            jax.ShapeDtypeStruct((30, rows, LANES), f32),
            jax.ShapeDtypeStruct((16, rows, LANES), f32),
        ),
        in_specs=[VMEM] * 7 + [SMEM] * 2,
        out_specs=(VMEM,) * 3,
        scratch_shapes=[
            pltpu.VMEM((8 * blocks, LANES), f32),
            pltpu.VMEM((WIDE * blocks, LANES), f32),
            pltpu.VMEM((7, sizes.tall, LANES), f32),
        ],
        compiler_params=PARAMS,
    )(state, depth, metric, partner, refine, before, after, diff_ops, lift)
    return pl.pallas_call(
        functools.partial(second_kernel, sizes),
        name="second_stage_refine",
        out_shape=jax.ShapeDtypeStruct((3, 10, LANES * slots), f32),
        in_specs=[VMEM] * 4 + [SMEM] * 2 + [VMEM],
        out_specs=VMEM,
        scratch_shapes=[
            pltpu.VMEM((30, sizes.tall, LANES), f32),
            pltpu.VMEM((slots + 8, LANES), f32),
            pltpu.VMEM((8, LANES), jnp.int32),
            pltpu.SMEM((8, LANES), jnp.int32),
            pltpu.VMEM((WIDE * (slots + 1), LANES), f32),
            pltpu.VMEM((2 * WIDE, WIDE), f32),
            pltpu.VMEM((WIDE, LANES * slots), f32),
            pltpu.VMEM((3, slots, LANES), f32),
            pltpu.SemaphoreType.DMA,
        ],
        compiler_params=PARAMS,
    )(cur, rates, geo, stats, diff_ops, lift, prolong)


def solution(mesh):
    return jax.shard_map(
        shards,
        mesh=mesh,
        in_specs=(
            P(None, None, AXES),
            P(AXES),
            P(None, AXES),
            P(AXES),
            P(AXES),
            P(),
            P(),
            P(),
        ),
        out_specs=P(None, None, AXES),
        check_vma=False,
    )
```

time: 695 us -> 34.4 us (0.05)
  the two profiles are of different devices: /device:TPU:4 before, /device:TPU:0 now
where the time goes in v1:
time: 34.4 us; the launch traced here: 33.7 us
  Pallas kernels  12.9 us (38%)
  local copies, waits for them, and re-layouts  11.1 us (32%)
  starting transfers between devices  9.56 us (28%)
    unnamed x35, local copies, waits for them, and re-layouts  9.65 us
    pallas_call x1, Pallas kernels, shards(): pl.pallas_call(functools.partial(second_kernel, sizes), name='second_stag...  8.19 us
    ppermute x1, starting transfers between devices, shards(): lax.ppermute(head, AXES, [((i + 1) % count, i) for i in range(count)])  5.92 us
    pallas_call x1, Pallas kernels, shards(): pl.pallas_call(functools.partial(first_kernel, sizes), name='first_stage'...  4.02 us
    all_to_all x1, starting transfers between devices, shards(): stats = lax.all_to_all(stats, AXES, 0, 0, tiled=True)  3.17 us
    pallas_call x1, local copies, waits for them, and re-layouts, shards(): pl.pallas_call(functools.partial(second_kernel, sizes), name='second_stag...  1.45 us
    pallas_call x1, Pallas kernels, shards(): pl.pallas_call(functools.partial(pack_kernel, sizes), name='pack', out_sh...  0.73 us
  transfers between devices with their start and end apart: 3, of which 0 were waited for; matrix products, arithmetic and copies ran while one was open for 2% of the time, Pallas kernels for 12%

profile of v1, /device:TPU:0, one launch (start us, length us, event | category | flops | bytes accessed | tf_op | source)
XLA Modules:
  0.0 33.7 jit_solution(11751948740936501210)
XLA Ops:
  0.0 0.0 copy-start
  0.0 0.0 copy-start.9
  0.0 0.0 copy-start.15
  0.0 1.5 %copy.16.state_ref = f32[3,10,4096]{2,1,0:T(8,128)S(1)} copy(f32[3,10,4096]{2,0,1:T(4,128)} %param.8) | data formatting | bytes 983040 | tf_op args[0]
  1.5 0.0 copy-done
  1.5 0.0 copy-done.9
  1.5 0.0 copy-done.7
  1.5 0.0 copy-done.6
  1.5 0.7 %pack.1 = (f32[32,128]{1,0:T(8,128)}, f32[360,128]{1,0:T(8,128)S(1)}, f32[360,128]{1,0:T(8,128)S(1)}) custom-call(f32[3,10,4096]{2,1,0:T(8,128)S(1)} %copy.16.state_ref, f32[32,128]{1,0:T(8,128)S(1)} %bitcast.7, f32[4,4096]{1,0:T(4,128)S(1)} %copy-done, s32[32,128]{1,0:T(8,128)S(1)} %bitcast.9, s32[32,128]{1,0:T(8,128)S(1)} %bitcast.11), custom_call_target="tpu_custom_call" | custom-call | tf_op jit(solution)/shard_map/pack/pallas_call | solution.py:356
  2.3 0.5 %collective-permute-start = (f32[360,128]{1,0:T(8,128)S(1)}, f32[360,128]{1,0:T(8,128)S(1)}, u32[]{:S(2)}, u32[]{:S(2)}) collective-permute-start(f32[360,128]{1,0:T(8,128)S(1)} %get-tuple-element.11), channel_id=1, source_target_pairs={{0,1},{1,2},{2,3},{3,4},{4,5},{5,6},{6,7},{7,8},{8,9},{9,10},{10,1... | collective-permute-start | bytes 552968 | tf_op jit(solution)/shard_map/ppermute | solution.py:365
  2.7 5.9 %collective-permute-start.1 = (f32[360,128]{1,0:T(8,128)S(1)}, f32[360,128]{1,0:T(8,128)S(1)}, u32[]{:S(2)}, u32[]{:S(2)}) collective-permute-start(f32[360,128]{1,0:T(8,128)S(1)} %get-tuple-element.12), channel_id=1, source_target_pairs={{1,0},{2,1},{3,2},{4,3},{5,4},{6,5},{7,6},{8,7},{9,8},{10,9},{11,1... | collective-permute-start | bytes 552968 | tf_op jit(solution)/shard_map/ppermute | solution.py:366
  8.6 3.2 %all-to-all-start = ((f32[32,1,128]{2,1,0:T(1,128)}), f32[32,1,128]{2,1,0:T(1,128)}, u32[]{:S(2)}, u32[]{:S(2)}) async-start(f32[32,1,128]{2,1,0:T(1,128)} %bitcast.4), calls=%async_computation | async-start | bytes 32768 | tf_op jit(solution)/shard_map/all_to_all | solution.py:367
  11.8 0.0 copy-done.14
  11.8 0.0 copy-done.15
  11.9 0.6 %copy.20.prolong_ref = f32[2,10,10]{2,1,0:T(8,128)} copy(f32[2,10,10]{2,0,1:T(2,128)S(1)} %copy-done.15) | data formatting | bytes 1600 | tf_op args[7]
  12.5 0.0 collective-permute-done.before_ref
  12.5 0.7 %copy-done.2 = f32[360,128]{1,0:T(8,128)} copy-done((f32[360,128]{1,0:T(8,128)}, f32[360,128]{1,0:T(8,128)S(1)}, u32[]{:S(2)}) %copy-start.2) | copy-done | bytes 184344
  13.1 0.0 collective-permute-done.1.after_ref
  13.1 0.7 %copy-done.4 = f32[360,128]{1,0:T(8,128)} copy-done((f32[360,128]{1,0:T(8,128)}, f32[360,128]{1,0:T(8,128)S(1)}, u32[]{:S(2)}) %copy-start.4) | copy-done | bytes 184344
  13.8 0.8 %copy-done.1 = f32[4,4096]{1,0:T(4,128)S(1)} copy-done((f32[4,4096]{1,0:T(4,128)S(1)}, f32[4,4096]{1,0:T(4,128)}, u32[]{:S(2)}) %copy-start.1) | copy-done | bytes 65560
  14.7 0.9 %copy-done.3 = f32[360,128]{1,0:T(8,128)S(1)} copy-done((f32[360,128]{1,0:T(8,128)S(1)}, f32[360,128]{1,0:T(8,128)}, u32[]{:S(2)}) %copy-start.3) | copy-done | bytes 184344
  15.6 0.9 %copy-done.5 = f32[360,128]{1,0:T(8,128)S(1)} copy-done((f32[360,128]{1,0:T(8,128)S(1)}, f32[360,128]{1,0:T(8,128)}, u32[]{:S(2)}) %copy-start.5) | copy-done | bytes 184344
  16.5 0.7 %copy-done.8 = s32[4096]{0:T(1024)S(1)} copy-done((s32[4096]{0:T(1024)S(1)}, s32[4096]{0:T(1024)}, u32[]{:S(2)}) %copy-start.8) | copy-done | bytes 16408
  17.2 0.7 %copy-done.10 = s32[4096]{0:T(1024)S(1)} copy-done((s32[4096]{0:T(1024)S(1)}, s32[4096]{0:T(1024)}, u32[]{:S(2)}) %copy-start.10) | copy-done | bytes 16408
  17.9 0.7 %copy-done.12 = f32[10,12]{1,0:T(8,128)S(1)} copy-done((f32[10,12]{1,0:T(8,128)S(1)}, f32[10,12]{1,0:T(8,128)}, u32[]{:S(2)}) %copy-start.12) | copy-done | bytes 504
  18.6 4.0 %first_stage.1 = (f32[30,80,128]{2,1,0:T(8,128)S(1)}, f32[30,64,128]{2,1,0:T(8,128)S(1)}, f32[16,64,128]{2,1,0:T(8,128)S(1)}) custom-call(f32[3,10,4096]{2,1,0:T(8,128)S(1)} %copy.16.state_ref, f32[32,128]{1,0:T(8,128)S(1)} %bitcast.8, f32[4,4096]{1,0:T(4,128)S(1)} %copy-done.1, s32[32,128]{1,0:T(8,128)S(1)} %bitcast.10, s32[32,128]{1,0:T(8,128)S(1)} %bitcast.12, ...), custom_call_target="tpu_custom_call" | custom-call | tf_op jit(solution)/shard_map/first_stage/pallas_call | solution.py:368
  22.7 0.0 all-to-all-done
  22.7 0.0 copy-start.11
  22.7 0.7 %copy-done.11 = f32[2,10,10]{2,1,0:T(8,128)S(1)} copy-done((f32[2,10,10]{2,1,0:T(8,128)S(1)}, f32[2,10,10]{2,1,0:T(8,128)}, u32[]{:S(2)}) %copy-start.11) | copy-done | bytes 824
  23.4 0.7 %copy-done.13 = f32[10,12]{1,0:T(8,128)S(1)} copy-done((f32[10,12]{1,0:T(8,128)S(1)}, f32[10,12]{1,0:T(8,128)}, u32[]{:S(2)}) %copy-start.13) | copy-done | bytes 504
  24.1 8.2 %second_stage_refine.1 = f32[3,10,6144]{2,1,0:T(8,128)S(1)} custom-call(f32[30,80,128]{2,1,0:T(8,128)S(1)} %get-tuple-element.13.cur, f32[30,64,128]{2,1,0:T(8,128)S(1)} %get-tuple-element.14.rate_ref, f32[16,64,128]{2,1,0:T(8,128)S(1)} %get-tuple-element.15.geo_ref, f32[32,128]{1,0:T(8,128)} %bitcast.5.stats_ref, f32[2,10,10]{2,1,0:T(8,128)S(1)} %copy.17.diff_ref, ...), custom_call_target="tpu_custom_call" | custom-call | tf_op jit(solution)/shard_map/second_stage_refine/pallas_call | solution.py:385
  32.3 1.5 %copy.21 = f32[3,10,6144]{2,0,1:T(4,128)} copy(f32[3,10,6144]{2,1,0:T(8,128)S(1)} %second_stage_refine.1) | data formatting | bytes 1474560 | tf_op jit(solution)/shard_map/second_stage_refine/pallas_call | solution.py:385
  (13 shorter events, 0.0 us)
Async XLA Ops:
  0.0 1.5 %copy-start = (f32[4,4096]{1,0:T(4,128)S(1)}, f32[4,4096]{1,0:T(4,128)}, u32[]{:S(2)}) copy-start(f32[4,4096]{1,0:T(4,128)} %metric_ref.3) | copy-start | bytes 196612
  0.0 1.5 %copy-start.9 = (s32[4096]{0:T(1024)S(1)}, s32[4096]{0:T(1024)}, u32[]{:S(2)}) copy-start(s32[4096]{0:T(1024)} %param.12) | copy-start | bytes 49156
  0.0 1.5 %copy-start.7 = (s32[4096]{0:T(1024)S(1)}, s32[4096]{0:T(1024)}, u32[]{:S(2)}) copy-start(s32[4096]{0:T(1024)} %param.11) | copy-start | bytes 49156
  0.0 1.5 %copy-start.6 = (f32[4096]{0:T(1024)S(1)}, f32[4096]{0:T(1024)}, u32[]{:S(2)}) copy-start(f32[4096]{0:T(1024)} %param.9) | copy-start | bytes 49156
  0.0 11.8 %copy-start.14 = (f32[2,10,10]{2,0,1:T(2,128)S(1)}, f32[2,10,10]{2,0,1:T(2,128)}, u32[]{:S(2)}) copy-start(f32[2,10,10]{2,0,1:T(2,128)} %param.13) | copy-start | bytes 2404
  0.0 11.8 %copy-start.15 = (f32[2,10,10]{2,0,1:T(2,128)S(1)}, f32[2,10,10]{2,0,1:T(2,128)}, u32[]{:S(2)}) copy-start(f32[2,10,10]{2,0,1:T(2,128)} %param.15) | copy-start | bytes 2404
  2.3 10.2 %collective-permute-start = (f32[360,128]{1,0:T(8,128)S(1)}, f32[360,128]{1,0:T(8,128)S(1)}, u32[]{:S(2)}, u32[]{:S(2)}) collective-permute-start(f32[360,128]{1,0:T(8,128)S(1)} %get-tuple-element.11), channel_id=1, source_target_pairs={{0,1},{1,2},{2,3},{3,4},{4,5},{5,6},{6,7},{7,8},{8,9},{9,10},{10,1... | collective-permute-start | bytes 552968 | tf_op jit(solution)/shard_map/ppermute | solution.py:365
  2.7 10.4 %collective-permute-start.1 = (f32[360,128]{1,0:T(8,128)S(1)}, f32[360,128]{1,0:T(8,128)S(1)}, u32[]{:S(2)}, u32[]{:S(2)}) collective-permute-start(f32[360,128]{1,0:T(8,128)S(1)} %get-tuple-element.12), channel_id=1, source_target_pairs={{1,0},{2,1},{3,2},{4,3},{5,4},{6,5},{7,6},{8,7},{9,8},{10,9},{11,1... | collective-permute-start | bytes 552968 | tf_op jit(solution)/shard_map/ppermute | solution.py:366
  8.6 14.0 %all-to-all-start = ((f32[32,1,128]{2,1,0:T(1,128)}), f32[32,1,128]{2,1,0:T(1,128)}, u32[]{:S(2)}, u32[]{:S(2)}) async-start(f32[32,1,128]{2,1,0:T(1,128)} %bitcast.4), calls=%async_computation | async-start | bytes 32768 | tf_op jit(solution)/shard_map/all_to_all | solution.py:367
  12.5 0.7 %copy-start.2 = (f32[360,128]{1,0:T(8,128)}, f32[360,128]{1,0:T(8,128)S(1)}, u32[]{:S(2)}) copy-start(f32[360,128]{1,0:T(8,128)S(1)} %collective-permute-done.before_ref) | copy-start | bytes 552964
  13.1 0.7 %copy-start.4 = (f32[360,128]{1,0:T(8,128)}, f32[360,128]{1,0:T(8,128)S(1)}, u32[]{:S(2)}) copy-start(f32[360,128]{1,0:T(8,128)S(1)} %collective-permute-done.1.after_ref) | copy-start | bytes 552964
  13.8 0.8 %copy-start.1 = (f32[4,4096]{1,0:T(4,128)S(1)}, f32[4,4096]{1,0:T(4,128)}, u32[]{:S(2)}) copy-start(f32[4,4096]{1,0:T(4,128)} %metric_ref.3) | copy-start | bytes 196612
  14.7 0.9 %copy-start.3 = (f32[360,128]{1,0:T(8,128)S(1)}, f32[360,128]{1,0:T(8,128)}, u32[]{:S(2)}) copy-start(f32[360,128]{1,0:T(8,128)} %copy-done.2) | copy-start | bytes 552964
  15.6 0.9 %copy-start.5 = (f32[360,128]{1,0:T(8,128)S(1)}, f32[360,128]{1,0:T(8,128)}, u32[]{:S(2)}) copy-start(f32[360,128]{1,0:T(8,128)} %copy-done.4) | copy-start | bytes 552964
  16.5 0.7 %copy-start.8 = (s32[4096]{0:T(1024)S(1)}, s32[4096]{0:T(1024)}, u32[]{:S(2)}) copy-start(s32[4096]{0:T(1024)} %param.11) | copy-start | bytes 49156
  17.2 0.7 %copy-start.10 = (s32[4096]{0:T(1024)S(1)}, s32[4096]{0:T(1024)}, u32[]{:S(2)}) copy-start(s32[4096]{0:T(1024)} %param.12) | copy-start | bytes 49156
  17.9 0.7 %copy-start.12 = (f32[10,12]{1,0:T(8,128)S(1)}, f32[10,12]{1,0:T(8,128)}, u32[]{:S(2)}) copy-start(f32[10,12]{1,0:T(8,128)} %lift_ref.3) | copy-start | bytes 1444
  22.7 0.7 %copy-start.11 = (f32[2,10,10]{2,1,0:T(8,128)S(1)}, f32[2,10,10]{2,1,0:T(8,128)}, u32[]{:S(2)}) copy-start(f32[2,10,10]{2,1,0:T(8,128)} %copy.20.prolong_ref) | copy-start | bytes 2404
  23.4 0.7 %copy-start.13 = (f32[10,12]{1,0:T(8,128)S(1)}, f32[10,12]{1,0:T(8,128)}, u32[]{:S(2)}) copy-start(f32[10,12]{1,0:T(8,128)} %lift_ref.3) | copy-start | bytes 1444
